TPU v7x, 32 devices: a whole 2x2x4 slice. The times are simulated.
32 devices in a mesh: grp: 8 (over z, y), seq: 4 (over x, core).
Axes of the slice: x: 2, y: 2, z: 4, core: 2. Of those that a mesh axis runs over, the one named last changes fastest.
Arguments:
- tokens_in: bfloat16 [24576, 768], P(('grp', 'seq')), may hold values from -6 to 6
- lengths: int32 [8], P('grp'), may hold values from 2305 to 3072, as said below
- ln1_gain: float32 [768], replicated, may hold values from 0.5 to 1.5
- ln1_bias: float32 [768], replicated, may hold values from -1.75 to 1.75
- w_qkv: bfloat16 [768, 2304], replicated, may hold values from -0.21875 to 0.21875
- bias_query: float32 [768], replicated, may hold values from -1.75 to 1.75
- bias_value: float32 [768], replicated, may hold values from -1.75 to 1.75
- w_out: bfloat16 [768, 768], replicated, may hold values from -0.875 to 0.875
- bias_out: float32 [768], replicated, may hold values from -1.75 to 1.75
- ln2_gain: float32 [768], replicated, may hold values from 0.5 to 1.5
- ln2_bias: float32 [768], replicated, may hold values from -1.75 to 1.75
- w_up: bfloat16 [768, 3072], replicated, may hold values from -0.21875 to 0.21875
- bias_up: float32 [3072], replicated, may hold values from -1.75 to 1.75
- w_down: bfloat16 [3072, 768], replicated, may hold values from -0.109375 to 0.109375
- bias_down: float32 [768], replicated, may hold values from -1.75 to 1.75
- proj_patch: bfloat16 [768, 768], replicated, may hold values from -0.21875 to 0.21875
- proj_class: bfloat16 [768, 768], replicated, may hold values from -0.21875 to 0.21875
- class_emb: bfloat16 [150, 768], replicated, may hold values from -6 to 6
- d_masks: bfloat16 [24576, 150], P(('grp', 'seq')), may hold values from -6 to 6
Outputs:
- masks: bfloat16 [24576, 150], P(('grp', 'seq'))
- grad_tokens: bfloat16 [24576, 768], P(('grp', 'seq'))
- grad_ln1_gain: float32 [768], P('grp')
- grad_ln1_bias: float32 [768], P('grp')
- grad_w_qkv: float32 [768, 2304], P('grp', 'seq')
- grad_bias_query: float32 [768], P('grp')
- grad_bias_value: float32 [768], P('grp')
- grad_w_out: float32 [768, 768], P('grp', 'seq')
- grad_bias_out: float32 [768], P('grp')
- grad_ln2_gain: float32 [768], P('grp')
- grad_ln2_bias: float32 [768], P('grp')
- grad_w_up: float32 [768, 3072], P('grp', 'seq')
- grad_bias_up: float32 [3072], P('grp')
- grad_w_down: float32 [3072, 768], P('grp', 'seq')
- grad_bias_down: float32 [768], P('grp')
- grad_proj_patch: float32 [768, 768], P('grp', 'seq')
- grad_proj_class: float32 [768, 768], P('grp', 'seq')
- grad_class_emb: float32 [150, 768], P(None, 'grp')
Inputs may be any that keep to these rules, and one draw needn't show every extreme that they name: Image g fills the first lengths[g] rows of its 3072 rows, the rest is padding; in every draw some image has exactly 3072 rows.
All inputs are finite; a program needn't handle non-finite values.
Results may differ from a plain program's by a relative error of at most 0.015.
Values may be sent and summed in bfloat16 or wider, within the bound.
A program may use at most 256 MiB of HBM per device.

v0:
```python
import math
import jax
import jax.numpy as jnp
from jax import lax
from jax.sharding import PartitionSpec as P

HEAD_DIM = 64
EPS_NORM = 1e-06
EPS_UNIT = 1e-06
NEG_FILL = -1e30


def layer_norm(matrix_rows, gain_vec, shift_vec):
    row_mean = jnp.mean(matrix_rows, axis=-1, keepdims=True)
    centred = matrix_rows - row_mean
    row_var = jnp.mean(centred * centred, axis=-1, keepdims=True)
    return centred * lax.rsqrt(row_var + EPS_NORM) * gain_vec + shift_vec


def unit_rows(matrix_rows):
    return matrix_rows * lax.rsqrt(
        jnp.sum(matrix_rows * matrix_rows, axis=-1, keepdims=True) + EPS_UNIT
    )


def gelu_exact(values_in):
    return jax.nn.gelu(values_in, approximate=False)


def score_block(query_heads, key_block, keep_block, score_scale):
    scores = (
        jnp.einsum("qhd,khd->hqk", query_heads, key_block, preferred_element_type=jnp.float32)
        * score_scale
    )
    return jnp.where(keep_block[None, None, :], scores, NEG_FILL)


def split_blocks(key_heads, value_heads, key_keep, key_span):
    block_count = key_heads.shape[0] // key_span
    head_count = key_heads.shape[1]
    key_blocks = key_heads.reshape(block_count, key_span, head_count, -1)
    value_blocks = value_heads.reshape(block_count, key_span, head_count, -1)
    keep_blocks = key_keep.reshape(block_count, key_span)
    return (key_blocks, value_blocks, keep_blocks)


def attend_forward(query_heads, key_heads, value_heads, key_keep, score_scale, key_span):
    row_count, head_count = (query_heads.shape[0], query_heads.shape[1])
    key_blocks, value_blocks, keep_blocks = split_blocks(key_heads, value_heads, key_keep, key_span)

    def gather_stats(carried, pieces):
        row_top, row_total = carried
        key_block, keep_block = pieces
        scores = score_block(query_heads, key_block, keep_block, score_scale)
        new_top = jnp.maximum(row_top, jnp.max(scores, axis=-1))
        row_total = row_total * jnp.exp(row_top - new_top) + jnp.sum(
            jnp.exp(scores - new_top[..., None]), axis=-1
        )
        return ((new_top, row_total), None)

    start_stats = (
        jnp.full((head_count, row_count), NEG_FILL, jnp.float32),
        jnp.zeros((head_count, row_count), jnp.float32),
    )
    row_top, row_total = lax.scan(gather_stats, start_stats, (key_blocks, keep_blocks))[0]
    log_mass = row_top + jnp.log(row_total)

    def weigh_values(summed, pieces):
        key_block, value_block, keep_block = pieces
        scores = score_block(query_heads, key_block, keep_block, score_scale)
        prob_low = jnp.exp(scores - log_mass[..., None]).astype(jnp.bfloat16)
        summed = summed + jnp.einsum(
            "hqk,khd->qhd", prob_low, value_block, preferred_element_type=jnp.float32
        )
        return (summed, None)

    start_sum = jnp.zeros(query_heads.shape, jnp.float32)
    attended = lax.scan(weigh_values, start_sum, (key_blocks, value_blocks, keep_blocks))[0]
    return (attended, log_mass)


def attend_backward(
    query_heads,
    key_heads,
    value_heads,
    key_keep,
    grad_heads,
    log_mass,
    attended,
    score_scale,
    key_span,
):
    head_count = query_heads.shape[1]
    key_blocks, value_blocks, keep_blocks = split_blocks(key_heads, value_heads, key_keep, key_span)
    row_delta = jnp.einsum("qhd,qhd->hq", grad_heads.astype(jnp.float32), attended)

    def spread_grads(grad_query, pieces):
        key_block, value_block, keep_block = pieces
        prob_rows = jnp.exp(
            score_block(query_heads, key_block, keep_block, score_scale) - log_mass[..., None]
        )
        grad_probs = jnp.einsum(
            "qhd,khd->hqk", grad_heads, value_block, preferred_element_type=jnp.float32
        )
        grad_scores = (prob_rows * (grad_probs - row_delta[..., None])).astype(jnp.bfloat16)
        grad_query = grad_query + jnp.einsum(
            "hqk,khd->qhd", grad_scores, key_block, preferred_element_type=jnp.float32
        )
        grad_key_block = (
            jnp.einsum("hqk,qhd->khd", grad_scores, query_heads, preferred_element_type=jnp.float32)
            * score_scale
        )
        grad_value_block = jnp.einsum(
            "hqk,qhd->khd",
            prob_rows.astype(jnp.bfloat16),
            grad_heads,
            preferred_element_type=jnp.float32,
        )
        return (grad_query, (grad_key_block, grad_value_block))

    start_query = jnp.zeros(query_heads.shape, jnp.float32)
    grad_query, block_grads = lax.scan(
        spread_grads, start_query, (key_blocks, value_blocks, keep_blocks)
    )
    total_rows = key_heads.shape[0]
    model_width = head_count * query_heads.shape[2]
    grad_key_all = block_grads[0].reshape(total_rows, model_width)
    grad_value_all = block_grads[1].reshape(total_rows, model_width)
    return (grad_query * score_scale, grad_key_all, grad_value_all)


def column_sum(matrix_low):
    return jnp.sum(matrix_low.astype(jnp.float32), axis=0)


def body(
    tokens_in,
    lengths,
    ln1_gain,
    ln1_bias,
    w_qkv,
    bias_query,
    bias_value,
    w_out,
    bias_out,
    ln2_gain,
    ln2_bias,
    w_up,
    bias_up,
    w_down,
    bias_down,
    proj_patch,
    proj_class,
    class_emb,
    d_masks,
):
    row_count, model_width = tokens_in.shape
    head_size = HEAD_DIM
    head_count = model_width // head_size
    seq_devices = lax.axis_size("seq")
    grp_devices = lax.axis_size("grp")
    seq_total = row_count * seq_devices
    key_span = min(512, seq_total)
    score_scale = head_size ** (-0.5)
    mask_scale = math.sqrt(model_width)
    length_here = lengths[0]
    first_row = lax.axis_index("seq") * row_count
    valid_rows = (first_row + jnp.arange(row_count, dtype=jnp.int32) < length_here).astype(
        jnp.float32
    )
    key_keep = jnp.arange(seq_total, dtype=jnp.int32) < length_here
    tokens = tokens_in.astype(jnp.float32)
    normed_one, norm_one_back = jax.vjp(layer_norm, tokens, ln1_gain, ln1_bias)
    normed_low = normed_one.astype(jnp.bfloat16)
    zero_keys = jnp.zeros_like(bias_query)
    mixed = jnp.dot(normed_low, w_qkv, preferred_element_type=jnp.float32)
    mixed = mixed + jnp.concatenate([bias_query, zero_keys, bias_value])
    mixed_low = mixed.astype(jnp.bfloat16)
    query_heads = mixed_low[:, :model_width].reshape(row_count, head_count, head_size)
    key_rows = mixed_low[:, model_width : 2 * model_width]
    value_rows = mixed_low[:, 2 * model_width :]
    key_all, value_all = (
        lax.all_gather(key_rows, "seq", axis=0, tiled=True),
        lax.all_gather(value_rows, "seq", axis=0, tiled=True),
    )
    key_heads = key_all.reshape(seq_total, head_count, head_size)
    value_heads = value_all.reshape(seq_total, head_count, head_size)
    attended, log_mass = attend_forward(
        query_heads, key_heads, value_heads, key_keep, score_scale, key_span
    )
    attended_low = attended.reshape(row_count, model_width).astype(jnp.bfloat16)
    branch = jnp.dot(attended_low, w_out, preferred_element_type=jnp.float32) + bias_out
    middle = tokens + branch
    normed_two, norm_two_back = jax.vjp(layer_norm, middle, ln2_gain, ln2_bias)
    normed_two_low = normed_two.astype(jnp.bfloat16)
    hidden = jnp.dot(normed_two_low, w_up, preferred_element_type=jnp.float32) + bias_up
    active, gelu_back = jax.vjp(gelu_exact, hidden)
    active_low = active.astype(jnp.bfloat16)
    final = middle + (jnp.dot(active_low, w_down, preferred_element_type=jnp.float32) + bias_down)
    final_low = final.astype(jnp.bfloat16)
    patches = jnp.dot(final_low, proj_patch, preferred_element_type=jnp.float32)
    patch_unit, patch_back = jax.vjp(unit_rows, patches)
    patch_low = patch_unit.astype(jnp.bfloat16)
    classes = jnp.dot(class_emb, proj_class, preferred_element_type=jnp.float32)
    class_unit, class_back = jax.vjp(unit_rows, classes)
    class_low = class_unit.astype(jnp.bfloat16)
    mask_out = jnp.einsum("rd,cd->rc", patch_low, class_low, preferred_element_type=jnp.float32)
    mask_out = (mask_out * mask_scale * valid_rows[:, None]).astype(jnp.bfloat16)
    mask_grad = (d_masks.astype(jnp.float32) * valid_rows[:, None]).astype(jnp.bfloat16)
    grad_patch_unit = jnp.dot(mask_grad, class_low, preferred_element_type=jnp.float32) * mask_scale
    class_part = (
        jnp.einsum("rc,rd->cd", mask_grad, patch_low, preferred_element_type=jnp.float32)
        * mask_scale
    )
    class_total = lax.psum(class_part, ("grp", "seq"))
    grad_classes = class_back(class_total)[0].astype(jnp.bfloat16)
    class_proj_full = jnp.einsum(
        "cd,ce->de", class_emb, grad_classes, preferred_element_type=jnp.float32
    )
    class_emb_full = jnp.einsum(
        "ce,de->cd", grad_classes, proj_class, preferred_element_type=jnp.float32
    )
    grad_patches = patch_back(grad_patch_unit)[0].astype(jnp.bfloat16)
    grad_proj_patch = jnp.einsum(
        "rd,re->de", final_low, grad_patches, preferred_element_type=jnp.float32
    )
    grad_final = jnp.einsum(
        "re,de->rd", grad_patches, proj_patch, preferred_element_type=jnp.float32
    )
    grad_feed = grad_final.astype(jnp.bfloat16)
    grad_w_down = jnp.einsum("rf,rd->fd", active_low, grad_feed, preferred_element_type=jnp.float32)
    grad_bias_down = column_sum(grad_feed)
    grad_active = jnp.einsum("rd,fd->rf", grad_feed, w_down, preferred_element_type=jnp.float32)
    grad_hidden = gelu_back(grad_active)[0].astype(jnp.bfloat16)
    grad_w_up = jnp.einsum(
        "rd,rf->df", normed_two_low, grad_hidden, preferred_element_type=jnp.float32
    )
    grad_bias_up = column_sum(grad_hidden)
    grad_normed_two = jnp.einsum("rf,df->rd", grad_hidden, w_up, preferred_element_type=jnp.float32)
    grad_middle_norm, grad_ln2_gain, grad_ln2_bias = norm_two_back(grad_normed_two)
    grad_middle = grad_final + grad_middle_norm
    grad_branch = grad_middle.astype(jnp.bfloat16)
    grad_w_out = jnp.einsum(
        "rd,re->de", attended_low, grad_branch, preferred_element_type=jnp.float32
    )
    grad_bias_out = column_sum(grad_branch)
    grad_attended = jnp.einsum("re,de->rd", grad_branch, w_out, preferred_element_type=jnp.float32)
    grad_heads = grad_attended.astype(jnp.bfloat16).reshape(row_count, head_count, head_size)
    grad_query, grad_key_all, grad_value_all = attend_backward(
        query_heads,
        key_heads,
        value_heads,
        key_keep,
        grad_heads,
        log_mass,
        attended,
        score_scale,
        key_span,
    )
    grad_key_own, grad_value_own = (
        lax.psum_scatter(
            grad_key_all.astype(jnp.bfloat16), "seq", scatter_dimension=0, tiled=True
        ).astype(jnp.float32),
        lax.psum_scatter(
            grad_value_all.astype(jnp.bfloat16), "seq", scatter_dimension=0, tiled=True
        ).astype(jnp.float32),
    )
    grad_mixed = jnp.concatenate(
        [grad_query.reshape(row_count, model_width), grad_key_own, grad_value_own], axis=1
    ).astype(jnp.bfloat16)
    grad_w_qkv = jnp.einsum("rd,rm->dm", normed_low, grad_mixed, preferred_element_type=jnp.float32)
    grad_bias_all = column_sum(grad_mixed)
    grad_bias_query = grad_bias_all[:model_width]
    grad_bias_value = grad_bias_all[2 * model_width :]
    grad_normed_one = jnp.einsum("rm,dm->rd", grad_mixed, w_qkv, preferred_element_type=jnp.float32)
    grad_tokens_norm, grad_ln1_gain, grad_ln1_bias = norm_one_back(grad_normed_one)
    grad_tokens = (grad_middle + grad_tokens_norm).astype(jnp.bfloat16)
    row_parts = (
        lax.psum_scatter(grad_w_qkv, "grp", scatter_dimension=0, tiled=True),
        lax.psum_scatter(grad_w_out, "grp", scatter_dimension=0, tiled=True),
        lax.psum_scatter(grad_w_up, "grp", scatter_dimension=0, tiled=True),
        lax.psum_scatter(grad_w_down, "grp", scatter_dimension=0, tiled=True),
        lax.psum_scatter(grad_proj_patch, "grp", scatter_dimension=0, tiled=True),
        lax.psum_scatter(grad_ln1_gain, "grp", scatter_dimension=0, tiled=True),
        lax.psum_scatter(grad_ln1_bias, "grp", scatter_dimension=0, tiled=True),
        lax.psum_scatter(grad_bias_query, "grp", scatter_dimension=0, tiled=True),
        lax.psum_scatter(grad_bias_value, "grp", scatter_dimension=0, tiled=True),
        lax.psum_scatter(grad_bias_out, "grp", scatter_dimension=0, tiled=True),
        lax.psum_scatter(grad_ln2_gain, "grp", scatter_dimension=0, tiled=True),
        lax.psum_scatter(grad_ln2_bias, "grp", scatter_dimension=0, tiled=True),
        lax.psum_scatter(grad_bias_up, "grp", scatter_dimension=0, tiled=True),
        lax.psum_scatter(grad_bias_down, "grp", scatter_dimension=0, tiled=True),
    )
    matrix_parts = (
        lax.psum_scatter(
            row_parts[0].astype(jnp.bfloat16), "seq", scatter_dimension=1, tiled=True
        ).astype(jnp.float32),
        lax.psum_scatter(
            row_parts[1].astype(jnp.bfloat16), "seq", scatter_dimension=1, tiled=True
        ).astype(jnp.float32),
        lax.psum_scatter(
            row_parts[2].astype(jnp.bfloat16), "seq", scatter_dimension=1, tiled=True
        ).astype(jnp.float32),
        lax.psum_scatter(
            row_parts[3].astype(jnp.bfloat16), "seq", scatter_dimension=1, tiled=True
        ).astype(jnp.float32),
        lax.psum_scatter(
            row_parts[4].astype(jnp.bfloat16), "seq", scatter_dimension=1, tiled=True
        ).astype(jnp.float32),
    )
    vector_parts = lax.psum(
        (
            row_parts[5],
            row_parts[6],
            row_parts[7],
            row_parts[8],
            row_parts[9],
            row_parts[10],
            row_parts[11],
            row_parts[12],
            row_parts[13],
        ),
        "seq",
    )
    rows_each = model_width // grp_devices
    cols_each = model_width // seq_devices
    grp_here = lax.axis_index("grp")
    seq_here = lax.axis_index("seq")
    grad_proj_class = lax.dynamic_slice(
        class_proj_full, (grp_here * rows_each, seq_here * cols_each), (rows_each, cols_each)
    )
    grad_class_emb = lax.dynamic_slice_in_dim(class_emb_full, grp_here * rows_each, rows_each, 1)
    return (
        mask_out,
        grad_tokens,
        vector_parts[0],
        vector_parts[1],
        matrix_parts[0],
        vector_parts[2],
        vector_parts[3],
        matrix_parts[1],
        vector_parts[4],
        vector_parts[5],
        vector_parts[6],
        matrix_parts[2],
        vector_parts[7],
        matrix_parts[3],
        vector_parts[8],
        matrix_parts[4],
        grad_proj_class,
        grad_class_emb,
    )


def solution(mesh):
    return jax.shard_map(
        body,
        mesh=mesh,
        in_specs=(
            P(("grp", "seq"), None),
            P("grp"),
            P(),
            P(),
            P(),
            P(),
            P(),
            P(),
            P(),
            P(),
            P(),
            P(),
            P(),
            P(),
            P(),
            P(),
            P(),
            P(),
            P(("grp", "seq"), None),
        ),
        out_specs=(
            P(("grp", "seq"), None),
            P(("grp", "seq"), None),
            P("grp"),
            P("grp"),
            P("grp", "seq"),
            P("grp"),
            P("grp"),
            P("grp", "seq"),
            P("grp"),
            P("grp"),
            P("grp"),
            P("grp", "seq"),
            P("grp"),
            P("grp", "seq"),
            P("grp"),
            P("grp", "seq"),
            P("grp", "seq"),
            P(None, "grp"),
        ),
        check_vma=False,
    )
```

profile of v0, /device:TPU:0, one launch (start us, length us, event | category | flops | bytes accessed | tf_op | source)
XLA Modules:
  0.0 1562.4 jit_solution(7666178320111044407)
XLA Ops:
  30.2 29.2 %all-gather.5.cloned.1.call-done = bf16[3072,768]{1,0:T(8,128)(2,1)} async-done(((bf16[768,768]{1,0:T(8,128)(2,1)}), bf16[3072,768]{1,0:T(8,128)(2,1)}) %all-gather.5.cloned.1.call-update) | async-done | bytes 4718608 | tf_op jit(solution)/shard_map/all_gather | solution.py:183
  59.4 15.0 reshape.189
  74.4 13.5 copy.80
  88.0 165.2 %while.39 = (s32[]{:T(128)}, f32[12,768]{1,0:T(8,128)}, f32[12,768]{1,0:T(8,128)}, pred[6,512]{1,0:T(8,128)(4,1)S(1)}, bf16[6,512,12,64]{1,3,2,0:T(8,128)(2,1)},...) while((s32[]{:T(128)}, f32[12,768]{1,0:T(8,128)}, f32[12,768]{1,0:T(8,128)}, ...), condition=%wide.region_5.6_spmd.clone, body=%wide.region_2.5_spmd.clone.sunk | while | flops 637056000 | bytes 40196704 | solution.py:65
  88.0 12.4 bitcast_reduce_fusion.2
  115.5 12.3 bitcast_reduce_fusion.2
  143.0 12.3 bitcast_reduce_fusion.2
  170.6 12.3 bitcast_reduce_fusion.2
  198.1 12.3 bitcast_reduce_fusion.2
  211.9 10.8 fusion.145
  225.6 12.3 bitcast_reduce_fusion.2
  253.2 15.0 reshape.188
  268.1 13.6 copy.79
  283.2 61.1 %while.40 = (s32[]{:T(128)}, f32[768,12,64]{0,2,1:T(8,128)}, bf16[6,512,12,64]{1,3,2,0:T(8,128)(2,1)}, pred[6,512]{1,0:T(8,128)(4,1)S(1)}, bf16[6,512,12,64]{1,3...) while((s32[]{:T(128)}, f32[768,12,64]{0,2,1:T(8,128)}, ...), condition=%wide.region_7.8_spmd.clone, body=%wide.region_6.7_spmd.clone.sunk | while | flops 1228013568 | bytes 7522923 | solution.py:78
  350.3 28.6 %multiply_convert_fusion.1 = (bf16[768,3072]{1,0:T(8,128)(2,1)S(1)}, f32[768,3072]{1,0:T(8,128)}, f32[768,3072]{1,0:T(8,128)}) fusion(f32[3072]{0:T(1024)S(1)} %copy-done.54, bf16[768,3072]{1,0:T(8,128)(2,1)S(1)} %bitcast.171, f32[768,768]{0,1:T(8,128)S(1)} %get-tuple-element.449, f32[768]{0:T(1024)S(1)} %copy-done.57, f32[768]{0:T(1024)S(1)} %copy-done.42, ...), kind=kOutput, calls=%fused_computation.51 | convolution fusion | flops 3782541312 | bytes 30695424 | tf_op jit(solution)/shard_map/dot_general | solution.py:196
  395.1 13.0 convert_reduce_fusion
  433.9 291.4 %while.41 = (s32[]{:T(128)}, f32[768,12,64]{0,2,1:T(8,128)}, bf16[6,512,12,64]{1,3,2,0:T(8,128)(2,1)}, bf16[6,512,12,64]{1,3,2,0:T(8,128)(2,1)}, bf16[6,512,12,6...) while((s32[]{:T(128)}, f32[768,12,64]{0,2,1:T(8,128)}, ...), condition=%wide.region_16.17_spmd.clone, body=%wide.region_15.16_spmd.clone.sunk | while | flops 3068657664 | bytes 142766832 | solution.py:122
  445.0 10.9 multiply_convert_fusion.13
  470.6 11.9 bitcast_dynamic-update-slice_fusion.5
  493.2 10.8 multiply_convert_fusion.13
  519.2 11.9 bitcast_dynamic-update-slice_fusion.5
  567.8 11.9 bitcast_dynamic-update-slice_fusion.5
  616.3 11.9 bitcast_dynamic-update-slice_fusion.5
  664.8 11.9 bitcast_dynamic-update-slice_fusion.5
  713.3 11.8 bitcast_dynamic-update-slice_fusion.5
  784.4 50.4 %reduce-scatter.23.cloned.1.call-done = bf16[768,768]{0,1:T(8,128)(2,1)} async-done(((bf16[3072,768]{0,1:T(8,128)(2,1)}), bf16[768,768]{0,1:T(8,128)(2,1)}) %reduce-scatter.23.cloned.1.call-update) | async-done | bytes 1179664 | tf_op jit(solution)/shard_map/reduce_scatter | solution.py:264
  848.8 118.0 %all-reduce.13.cloned.1.call-done = f32[150,768]{1,0:T(8,128)} async-done(((f32[150,768]{1,0:T(8,128)}), f32[150,768]{1,0:T(8,128)}) %all-reduce.13.cloned.1.call-update) | async-done | bytes 460816 | tf_op jit(solution)/shard_map/psum | solution.py:215
  968.6 165.9 %reduce-scatter.33.cloned.1.call-done = f32[384,768]{1,0:T(8,128)} async-done(((f32[3072,768]{1,0:T(8,128)}), f32[384,768]{1,0:T(8,128)}) %reduce-scatter.33.cloned.1.call-update) | async-done | bytes 1179664 | tf_op jit(solution)/shard_map/reduce_scatter | solution.py:282
  1159.6 19.8 %reduce-scatter.39.cloned.1.call-done = bf16[192,96]{1,0:T(8,128)(2,1)} async-done(((bf16[768,96]{1,0:T(8,128)(2,1)}), bf16[192,96]{1,0:T(8,128)(2,1)}) %reduce-scatter.39.cloned.1.call-update) | async-done | bytes 36880
  1182.3 164.4 %reduce-scatter.29.cloned.1.call-done = f32[96,3072]{1,0:T(8,128)} async-done(((f32[768,3072]{1,0:T(8,128)}), f32[96,3072]{1,0:T(8,128)}) %reduce-scatter.29.cloned.1.call-update) | async-done | bytes 1179664 | tf_op jit(solution)/shard_map/reduce_scatter | solution.py:281
  1366.1 112.8 %reduce-scatter.25.cloned.1.call-done = f32[96,2304]{1,0:T(8,128)} async-done(((f32[768,2304]{1,0:T(8,128)}), f32[96,2304]{1,0:T(8,128)}) %reduce-scatter.25.cloned.1.call-update) | async-done | bytes 884752 | tf_op jit(solution)/shard_map/reduce_scatter | solution.py:279
  1484.3 36.8 %all-reduce.9 = (f32[768]{0:T(1024)}, f32[768]{0:T(1024)}, f32[768]{0:T(1024)}, f32[768]{0:T(1024)}, f32[768]{0:T(1024)}, /*index=5*/f32[768]{0:T(1024)}, f32[768]{0:T(1024)}, f32[3072]{0:T(1024)}, f32[768]{0:T(1024)}) all-reduce(f32[768]{0:T(1024)} %get-tuple-element.362, ...), channel_id=4, replica_groups=mesh['grp'=8,'seq'=4] {'grp'}, use_global_device_ids=true, to_apply=%region_22.23.clone | all-reduce | flops 9216 | bytes 73728
  (381 shorter events, 570.3 us)
Async XLA Ops:
  7.2 52.1 %all-gather.5.cloned.1.call-start = ((), (), s32[]{:S(2)}) async-start(), calls=%async_computation.13 | async-start | bytes 5898240 | tf_op jit(solution)/shard_map/all_gather | solution.py:183
  19.1 234.1 %all-gather.3.cloned.1.call-start = ((), (), s32[]{:S(2)}) async-start(), calls=%async_computation.12 | async-start | bytes 5898240 | tf_op jit(solution)/shard_map/all_gather | solution.py:184
  19.8 742.3 %reduce-scatter.35.cloned.1.call-start = ((), (), s32[]{:S(2)}) async-start(), calls=%async_computation.21 | async-start | bytes 2654208 | tf_op jit(solution)/shard_map/reduce_scatter | solution.py:283
  26.3 48.1 %copy-start.40 = (f32[150]{0:T(256)}, f32[150]{0:T(256)S(1)}, u32[]{:S(2)}) copy-start(f32[150]{0:T(256)S(1)} %add_rsqrt_fusion.1) | copy-start | bytes 1804
  346.6 32.3 %slice-start = ((s8[4718592]{0:T(1024)(128)(4,1)}), s8[4194304]{0:T(1024)(128)(4,1)S(1)}, s32[]{:S(2)}) async-start(s8[4718592]{0:T(1024)(128)(4,1)} %bitcast.168), calls=%async_computation.27 | async-start | bytes 8388608
  347.9 31.0 %copy-start.7 = (f32[768,768]{0,1:T(8,128)}, f32[768,768]{0,1:T(8,128)S(1)}, u32[]{:S(2)}) copy-start(f32[768,768]{0,1:T(8,128)S(1)} %get-tuple-element.449) | copy-start | bytes 7077892
  348.0 77.0 %copy-start.24 = (f32[768]{0:T(1024)}, f32[768]{0:T(1024)S(1)}, u32[]{:S(2)}) copy-start(f32[768]{0:T(1024)S(1)} %broadcast_multiply_fusion.1) | copy-start | bytes 9220
  350.3 74.7 %copy-start.38 = (f32[768]{0:T(1024)}, f32[768]{0:T(1024)S(1)}, u32[]{:S(2)}) copy-start(f32[768]{0:T(1024)S(1)} %fusion.66) | copy-start | bytes 9220
  350.3 28.7 %slice-start.1 = ((s8[4718592]{0:T(1024)(128)(4,1)}), s8[524288]{0:T(1024)(128)(4,1)S(1)}, s32[]{:S(2)}) async-start(s8[4718592]{0:T(1024)(128)(4,1)} %bitcast.168), calls=%async_computation.28 | async-start | bytes 1048576
  350.3 28.7 %copy-start.56 = (f32[768]{0:T(1024)S(1)}, f32[768]{0:T(1024)}, u32[]{:S(2)}) copy-start(f32[768]{0:T(1024)} %param.39) | copy-start | bytes 9220
  391.7 373.9 %reduce-scatter.27.cloned.1.call-start = ((), (), s32[]{:S(2)}) async-start(), calls=%async_computation.17 | async-start | bytes 2654208 | tf_op jit(solution)/shard_map/reduce_scatter | solution.py:280
  433.8 350.6 %reduce-scatter.21.cloned.1.call-start = ((), (), s32[]{:S(2)}) async-start(), calls=%async_computation.14 | async-start | bytes 5898240 | tf_op jit(solution)/shard_map/reduce_scatter | solution.py:261
  445.0 14.6 copy-start.2
  493.2 14.5 copy-start.2
  541.8 14.4 copy-start.2
  590.4 14.4 copy-start.2
  638.8 14.4 copy-start.2
  687.3 14.4 copy-start.2
  736.2 98.6 %reduce-scatter.23.cloned.1.call-start = ((), (), s32[]{:S(2)}) async-start(), calls=%async_computation.15 | async-start | bytes 5898240 | tf_op jit(solution)/shard_map/reduce_scatter | solution.py:264
  747.4 219.4 %all-reduce.13.cloned.1.call-start = ((), (), s32[]{:S(2)}) async-start(), calls=%async_computation.22 | async-start | bytes 933888 | tf_op jit(solution)/shard_map/psum | solution.py:215
  751.3 383.3 %reduce-scatter.33.cloned.1.call-start = ((), (), s32[]{:S(2)}) async-start(), calls=%async_computation.20 | async-start | bytes 10616832 | tf_op jit(solution)/shard_map/reduce_scatter | solution.py:282
  762.0 394.6 %reduce-scatter.43.cloned.1.call-start = ((), (), s32[]{:S(2)}) async-start(), calls=%async_computation.26 | async-start | bytes 245760
  765.5 413.9 %reduce-scatter.39.cloned.1.call-start = ((), (), s32[]{:S(2)}) async-start(), calls=%async_computation.24 | async-start | bytes 245760
  769.0 577.8 %reduce-scatter.29.cloned.1.call-start = ((), (), s32[]{:S(2)}) async-start(), calls=%async_computation.18 | async-start | bytes 10616832 | tf_op jit(solution)/shard_map/reduce_scatter | solution.py:281
  780.0 54.9 %copy-start.23 = (f32[768]{0:T(1024)S(1)}, f32[768]{0:T(1024)}, u32[]{:S(2)}) copy-start(f32[768]{0:T(1024)} %copy-done.22) | copy-start | bytes 9220
  780.0 54.9 %copy-start.32 = (f32[768]{0:T(1024)S(1)}, f32[768]{0:T(1024)}, u32[]{:S(2)}) copy-start(f32[768]{0:T(1024)} %copy-done.31) | copy-start | bytes 9220
  780.0 54.9 %copy-start.36 = (f32[768]{0:T(1024)S(1)}, f32[768]{0:T(1024)}, u32[]{:S(2)}) copy-start(f32[768]{0:T(1024)} %param.27) | copy-start | bytes 9220
  780.0 698.9 %reduce-scatter.25.cloned.1.call-start = ((), (), s32[]{:S(2)}) async-start(), calls=%async_computation.16 | async-start | bytes 7962624 | tf_op jit(solution)/shard_map/reduce_scatter | solution.py:279
  843.3 703.7 %reduce-scatter.41.cloned.1.call-start = ((), (), s32[]{:S(2)}) async-start(), calls=%async_computation.25 | async-start | bytes 737280
  848.8 290.8 %copy-start.41 = (f32[150]{0:T(256)S(1)}, f32[150]{0:T(256)}, u32[]{:S(2)}) copy-start(f32[150]{0:T(256)} %copy-done.40) | copy-start | bytes 1804
  1138.9 411.6 %reduce-scatter.31.cloned.1.call-start = ((), (), s32[]{:S(2)}) async-start(), calls=%async_computation.19 | async-start | bytes 737280 | tf_op jit(solution)/shard_map/reduce_scatter | solution.py:301
  1348.9 203.2 %reduce-scatter.37.cloned.1.call-start = ((), (), s32[]{:S(2)}) async-start(), calls=%async_computation.23 | async-start | bytes 737280
  (68 other events, 315.5 us)
Sparse Core Ops, SparseCore 0:
  19.2 40.1 all-gather.4
  60.9 37.4 all-gather.2
  391.8 69.1 reduce-scatter.34
  464.4 68.0 reduce-scatter.26
  736.4 48.0 reduce-scatter.20
  787.0 47.8 reduce-scatter.22
  840.2 126.5 all-reduce.12
  970.8 163.7 reduce-scatter.32
  1137.7 18.8 reduce-scatter.42
  1159.6 19.7 reduce-scatter.38
  1183.4 163.2 reduce-scatter.28
  1350.7 128.1 reduce-scatter.24
  1481.4 21.1 reduce-scatter.40
  1504.9 22.0 reduce-scatter.30
  1529.4 22.0 reduce-scatter.36
where the time goes:
time: 1570 us; the launch traced here: 1560 us
  waiting for transfers between devices  671 us (43%)
  matrix products  526 us (34%)
  local copies, waits for them, and re-layouts  171 us (11%)
  other arithmetic  131 us (8%)
  blocking collectives  43.3 us (3%)
  between operations  17.1 us (1%)
    reduce_scatter x1, waiting for transfers between devices, body(): lax.psum_scatter(grad_w_down, 'grp', scatter_dimension=0, tiled=True)  166 us
    reduce_scatter x1, waiting for transfers between devices, body(): lax.psum_scatter(grad_w_up, 'grp', scatter_dimension=0, tiled=True)  164 us
    dot_general x12, matrix products, score_block(): jnp.einsum('qhd,khd->hqk', query_heads, key_block, preferred_element_type...  138 us
    psum x1, waiting for transfers between devices, body(): class_total = lax.psum(class_part, ('grp', 'seq'))  118 us
    reduce_scatter x1, waiting for transfers between devices, body(): lax.psum_scatter(grad_w_qkv, 'grp', scatter_dimension=0, tiled=True)  113 us
    unnamed x148, local copies, waits for them, and re-layouts  81.5 us
    dot_general x6, matrix products, spread_grads(): jnp.einsum('hqk,qhd->khd', prob_rows.astype(jnp.bfloat16), grad_heads, pr...  71.3 us
    reduce_sum x6, other arithmetic, gather_stats(): jnp.sum(jnp.exp(scores - new_top[..., None]), axis=-1)  64.9 us
  transfers between devices with their start and end apart: 15, of which 9 were waited for; matrix products, arithmetic and copies ran while one was open for 41% of the time, Pallas kernels for 0%

commit v1 on v0

--- a/solution.py
+++ b/solution.py
@@ -212,7 +212,7 @@
         jnp.einsum("rc,rd->cd", mask_grad, patch_low, preferred_element_type=jnp.float32)
         * mask_scale
     )
-    class_total = lax.psum(class_part, ("grp", "seq"))
+    class_total = lax.psum(lax.psum(class_part, "seq"), "grp")
     grad_classes = class_back(class_total)[0].astype(jnp.bfloat16)
     class_proj_full = jnp.einsum(
         "cd,ce->de", class_emb, grad_classes, preferred_element_type=jnp.float32

time: 1570 us -> 1520 us (0.968)
  waiting for transfers between devices: 671 us -> 616 us
    psum x1 -> x2, waiting for transfers between devices: 118 us -> 61.8 us  [body(): class_total = lax.psum(lax.psum(class_part, 'seq'), 'grp')]
    unnamed x148 -> x162, local copies, waits for them, and re-layouts: 81.5 us -> 82 us
  transfers between devices with their start and end apart: 15 -> 16, of which waited for: 9 -> 9; matrix products, arithmetic and copies ran while one was open for 41% -> 43% of each run, Pallas kernels for 0% -> 0%
where the time goes in v1:
time: 1520 us; the launch traced here: 1510 us
  waiting for transfers between devices  616 us (41%)
  matrix products  527 us (35%)
  local copies, waits for them, and re-layouts  171 us (11%)
  other arithmetic  134 us (9%)
  blocking collectives  43.3 us (3%)
  between operations  17.2 us (1%)
    reduce_scatter x1, waiting for transfers between devices, body(): lax.psum_scatter(grad_w_down, 'grp', scatter_dimension=0, tiled=True)  164 us
    reduce_scatter x1, waiting for transfers between devices, body(): lax.psum_scatter(grad_w_up, 'grp', scatter_dimension=0, tiled=True)  164 us
    dot_general x12, matrix products, score_block(): jnp.einsum('qhd,khd->hqk', query_heads, key_block, preferred_element_type...  138 us
    reduce_scatter x1, waiting for transfers between devices, body(): lax.psum_scatter(grad_w_qkv, 'grp', scatter_dimension=0, tiled=True)  113 us
    unnamed x162, local copies, waits for them, and re-layouts  82 us
    dot_general x6, matrix products, spread_grads(): jnp.einsum('hqk,qhd->khd', prob_rows.astype(jnp.bfloat16), grad_heads, pr...  71.6 us
    reduce_sum x6, other arithmetic, gather_stats(): jnp.sum(jnp.exp(scores - new_top[..., None]), axis=-1)  64.9 us
    dot_general x6, matrix products, spread_grads(): jnp.einsum('qhd,khd->hqk', grad_heads, value_block, preferred_element_typ...  64.5 us
  transfers between devices with their start and end apart: 16, of which 9 were waited for; matrix products, arithmetic and copies ran while one was open for 43% of the time, Pallas kernels for 0%

profile of v1, /device:TPU:0, one launch (start us, length us, event | category | flops | bytes accessed | tf_op | source)
XLA Modules:
  0.0 1511.1 jit_solution(10854293935117365652)
XLA Ops:
  30.2 29.2 %all-gather.5.cloned.1.call-done = bf16[3072,768]{1,0:T(8,128)(2,1)} async-done(((bf16[768,768]{1,0:T(8,128)(2,1)}), bf16[3072,768]{1,0:T(8,128)(2,1)}) %all-gather.5.cloned.1.call-update) | async-done | bytes 4718608 | tf_op jit(solution)/shard_map/all_gather | solution.py:183
  59.4 15.0 reshape.189
  74.4 13.5 copy.80
  88.0 165.3 %while.39 = (s32[]{:T(128)}, f32[12,768]{1,0:T(8,128)}, f32[12,768]{1,0:T(8,128)}, pred[6,512]{1,0:T(8,128)(4,1)S(1)}, bf16[6,512,12,64]{1,3,2,0:T(8,128)(2,1)},...) while((s32[]{:T(128)}, f32[12,768]{1,0:T(8,128)}, f32[12,768]{1,0:T(8,128)}, ...), condition=%wide.region_5.6_spmd.clone, body=%wide.region_2.5_spmd.clone.sunk | while | flops 637056000 | bytes 40196704 | solution.py:65
  88.0 12.4 bitcast_reduce_fusion.2
  101.8 10.8 fusion.145
  115.5 12.3 bitcast_reduce_fusion.2
  143.1 12.3 bitcast_reduce_fusion.2
  170.6 12.3 bitcast_reduce_fusion.2
  198.2 12.3 bitcast_reduce_fusion.2
  225.8 12.3 bitcast_reduce_fusion.2
  253.3 15.0 reshape.188
  268.3 13.6 copy.79
  283.3 61.1 %while.40 = (s32[]{:T(128)}, f32[768,12,64]{0,2,1:T(8,128)}, bf16[6,512,12,64]{1,3,2,0:T(8,128)(2,1)}, pred[6,512]{1,0:T(8,128)(4,1)S(1)}, bf16[6,512,12,64]{1,3...) while((s32[]{:T(128)}, f32[768,12,64]{0,2,1:T(8,128)}, ...), condition=%wide.region_7.8_spmd.clone, body=%wide.region_6.7_spmd.clone.sunk | while | flops 1228013568 | bytes 7522923 | solution.py:78
  350.5 28.6 %multiply_convert_fusion.1 = (bf16[768,3072]{1,0:T(8,128)(2,1)S(1)}, f32[768,3072]{1,0:T(8,128)}, f32[768,3072]{1,0:T(8,128)}) fusion(f32[3072]{0:T(1024)S(1)} %copy-done.58, bf16[768,3072]{1,0:T(8,128)(2,1)S(1)} %bitcast.171, f32[768,768]{0,1:T(8,128)S(1)} %get-tuple-element.449, f32[768]{0:T(1024)S(1)} %copy-done.61, f32[768]{0:T(1024)S(1)} %copy-done.45, ...), kind=kOutput, calls=%fused_computation.51 | convolution fusion | flops 3782541312 | bytes 30695424 | tf_op jit(solution)/shard_map/dot_general | solution.py:196
  401.0 13.0 convert_reduce_fusion
  440.2 292.5 %while.41 = (s32[]{:T(128)}, f32[768,12,64]{0,2,1:T(8,128)}, bf16[6,512,12,64]{1,3,2,0:T(8,128)(2,1)}, bf16[6,512,12,64]{1,3,2,0:T(8,128)(2,1)}, bf16[6,512,12,6...) while((s32[]{:T(128)}, f32[768,12,64]{0,2,1:T(8,128)}, ...), condition=%wide.region_16.17_spmd.clone, body=%wide.region_15.16_spmd.clone.sunk | while | flops 3068657664 | bytes 142766832 | solution.py:122
  476.9 12.1 bitcast_dynamic-update-slice_fusion.5
  499.7 10.8 multiply_convert_fusion.13
  525.9 12.1 bitcast_dynamic-update-slice_fusion.5
  548.7 10.9 multiply_convert_fusion.13
  574.9 11.9 bitcast_dynamic-update-slice_fusion.5
  623.4 11.9 bitcast_dynamic-update-slice_fusion.5
  672.1 11.9 bitcast_dynamic-update-slice_fusion.5
  720.7 11.9 bitcast_dynamic-update-slice_fusion.5
  791.6 50.4 %reduce-scatter.23.cloned.1.call-done = bf16[768,768]{0,1:T(8,128)(2,1)} async-done(((bf16[3072,768]{0,1:T(8,128)(2,1)}), bf16[768,768]{0,1:T(8,128)(2,1)}) %reduce-scatter.23.cloned.1.call-update) | async-done | bytes 1179664 | tf_op jit(solution)/shard_map/reduce_scatter | solution.py:264
  856.0 61.8 %all-reduce.16.cloned.1.call-done = f32[150,768]{1,0:T(8,128)} async-done(((f32[150,768]{1,0:T(8,128)}), f32[150,768]{1,0:T(8,128)}) %all-reduce.16.cloned.1.call-update) | async-done | bytes 460816 | tf_op jit(solution)/shard_map/psum | solution.py:215
  919.7 164.5 %reduce-scatter.33.cloned.1.call-done = f32[384,768]{1,0:T(8,128)} async-done(((f32[3072,768]{1,0:T(8,128)}), f32[384,768]{1,0:T(8,128)}) %reduce-scatter.33.cloned.1.call-update) | async-done | bytes 1179664 | tf_op jit(solution)/shard_map/reduce_scatter | solution.py:282
  1108.8 19.8 %reduce-scatter.39.cloned.1.call-done = bf16[192,96]{1,0:T(8,128)(2,1)} async-done(((bf16[768,96]{1,0:T(8,128)(2,1)}), bf16[192,96]{1,0:T(8,128)(2,1)}) %reduce-scatter.39.cloned.1.call-update) | async-done | bytes 36880
  1131.6 164.0 %reduce-scatter.29.cloned.1.call-done = f32[96,3072]{1,0:T(8,128)} async-done(((f32[768,3072]{1,0:T(8,128)}), f32[96,3072]{1,0:T(8,128)}) %reduce-scatter.29.cloned.1.call-update) | async-done | bytes 1179664 | tf_op jit(solution)/shard_map/reduce_scatter | solution.py:281
  1314.8 112.7 %reduce-scatter.25.cloned.1.call-done = f32[96,2304]{1,0:T(8,128)} async-done(((f32[768,2304]{1,0:T(8,128)}), f32[96,2304]{1,0:T(8,128)}) %reduce-scatter.25.cloned.1.call-update) | async-done | bytes 884752 | tf_op jit(solution)/shard_map/reduce_scatter | solution.py:279
  1432.9 36.8 %all-reduce.9 = (f32[768]{0:T(1024)}, f32[768]{0:T(1024)}, f32[768]{0:T(1024)}, f32[768]{0:T(1024)}, f32[768]{0:T(1024)}, /*index=5*/f32[768]{0:T(1024)}, f32[768]{0:T(1024)}, f32[3072]{0:T(1024)}, f32[768]{0:T(1024)}) all-reduce(f32[768]{0:T(1024)} %get-tuple-element.362, ...), channel_id=4, replica_groups=mesh['grp'=8,'seq'=4] {'grp'}, use_global_device_ids=true, to_apply=%region_22.23.clone | all-reduce | flops 9216 | bytes 73728
  (398 shorter events, 576.5 us)
Async XLA Ops:
  7.2 52.2 %all-gather.5.cloned.1.call-start = ((), (), s32[]{:S(2)}) async-start(), calls=%async_computation.13 | async-start | bytes 5898240 | tf_op jit(solution)/shard_map/all_gather | solution.py:183
  19.1 234.2 %all-gather.3.cloned.1.call-start = ((), (), s32[]{:S(2)}) async-start(), calls=%async_computation.12 | async-start | bytes 5898240 | tf_op jit(solution)/shard_map/all_gather | solution.py:184
  19.8 735.1 %all-reduce.14.cloned.1.call-start = ((), (), s32[]{:S(2)}) async-start(), calls=%async_computation.22 | async-start | bytes 933888 | tf_op jit(solution)/shard_map/psum | solution.py:215
  26.3 48.2 %copy-start.43 = (f32[150]{0:T(256)}, f32[150]{0:T(256)S(1)}, u32[]{:S(2)}) copy-start(f32[150]{0:T(256)S(1)} %add_rsqrt_fusion.1) | copy-start | bytes 1804
  346.8 32.3 %slice-start = ((s8[4718592]{0:T(1024)(128)(4,1)}), s8[4194304]{0:T(1024)(128)(4,1)S(1)}, s32[]{:S(2)}) async-start(s8[4718592]{0:T(1024)(128)(4,1)} %bitcast.168), calls=%async_computation.28 | async-start | bytes 8388608
  348.1 31.0 %copy-start.7 = (f32[768,768]{0,1:T(8,128)}, f32[768,768]{0,1:T(8,128)S(1)}, u32[]{:S(2)}) copy-start(f32[768,768]{0,1:T(8,128)S(1)} %get-tuple-element.449) | copy-start | bytes 7077892
  348.1 82.7 %copy-start.26 = (f32[768]{0:T(1024)}, f32[768]{0:T(1024)S(1)}, u32[]{:S(2)}) copy-start(f32[768]{0:T(1024)S(1)} %broadcast_multiply_fusion.1) | copy-start | bytes 9220
  350.4 80.4 %copy-start.41 = (f32[768]{0:T(1024)}, f32[768]{0:T(1024)S(1)}, u32[]{:S(2)}) copy-start(f32[768]{0:T(1024)S(1)} %fusion.66) | copy-start | bytes 9220
  350.5 28.7 %slice-start.1 = ((s8[4718592]{0:T(1024)(128)(4,1)}), s8[524288]{0:T(1024)(128)(4,1)S(1)}, s32[]{:S(2)}) async-start(s8[4718592]{0:T(1024)(128)(4,1)} %bitcast.168), calls=%async_computation.29 | async-start | bytes 1048576
  350.5 28.7 %copy-start.60 = (f32[768]{0:T(1024)S(1)}, f32[768]{0:T(1024)}, u32[]{:S(2)}) copy-start(f32[768]{0:T(1024)} %param.39) | copy-start | bytes 9220
  387.6 378.9 %reduce-scatter.35.cloned.1.call-start = ((), (), s32[]{:S(2)}) async-start(), calls=%async_computation.21 | async-start | bytes 2654208 | tf_op jit(solution)/shard_map/reduce_scatter | solution.py:283
  400.9 369.0 %reduce-scatter.27.cloned.1.call-start = ((), (), s32[]{:S(2)}) async-start(), calls=%async_computation.17 | async-start | bytes 2654208 | tf_op jit(solution)/shard_map/reduce_scatter | solution.py:280
  440.1 351.4 %reduce-scatter.21.cloned.1.call-start = ((), (), s32[]{:S(2)}) async-start(), calls=%async_computation.14 | async-start | bytes 5898240 | tf_op jit(solution)/shard_map/reduce_scatter | solution.py:261
  451.4 14.5 copy-start.2
  499.6 14.6 copy-start.2
  548.7 14.6 copy-start.2
  646.0 14.4 copy-start.2
  743.9 98.1 %reduce-scatter.23.cloned.1.call-start = ((), (), s32[]{:S(2)}) async-start(), calls=%async_computation.15 | async-start | bytes 5898240 | tf_op jit(solution)/shard_map/reduce_scatter | solution.py:264
  754.9 162.9 %all-reduce.16.cloned.1.call-start = ((), (), s32[]{:S(2)}) async-start(), calls=%async_computation.23 | async-start | bytes 933888 | tf_op jit(solution)/shard_map/psum | solution.py:215
  755.6 328.5 %reduce-scatter.33.cloned.1.call-start = ((), (), s32[]{:S(2)}) async-start(), calls=%async_computation.20 | async-start | bytes 10616832 | tf_op jit(solution)/shard_map/reduce_scatter | solution.py:282
  766.4 339.5 %reduce-scatter.43.cloned.1.call-start = ((), (), s32[]{:S(2)}) async-start(), calls=%async_computation.27 | async-start | bytes 245760
  769.9 358.8 %reduce-scatter.39.cloned.1.call-start = ((), (), s32[]{:S(2)}) async-start(), calls=%async_computation.25 | async-start | bytes 245760
  773.3 522.3 %reduce-scatter.29.cloned.1.call-start = ((), (), s32[]{:S(2)}) async-start(), calls=%async_computation.18 | async-start | bytes 10616832 | tf_op jit(solution)/shard_map/reduce_scatter | solution.py:281
  784.3 57.7 %copy-start.25 = (f32[768]{0:T(1024)S(1)}, f32[768]{0:T(1024)}, u32[]{:S(2)}) copy-start(f32[768]{0:T(1024)} %copy-done.24) | copy-start | bytes 9220
  784.3 57.7 %copy-start.35 = (f32[768]{0:T(1024)S(1)}, f32[768]{0:T(1024)}, u32[]{:S(2)}) copy-start(f32[768]{0:T(1024)} %copy-done.34) | copy-start | bytes 9220
  784.3 57.7 %copy-start.39 = (f32[768]{0:T(1024)S(1)}, f32[768]{0:T(1024)}, u32[]{:S(2)}) copy-start(f32[768]{0:T(1024)} %param.27) | copy-start | bytes 9220
  784.3 57.7 %copy-start.64 = (f32[768]{0:T(1024)S(1)}, f32[768]{0:T(1024)}, u32[]{:S(2)}) copy-start(f32[768]{0:T(1024)} %param.28) | copy-start | bytes 9220
  784.3 643.1 %reduce-scatter.25.cloned.1.call-start = ((), (), s32[]{:S(2)}) async-start(), calls=%async_computation.16 | async-start | bytes 7962624 | tf_op jit(solution)/shard_map/reduce_scatter | solution.py:279
  850.4 645.3 %reduce-scatter.41.cloned.1.call-start = ((), (), s32[]{:S(2)}) async-start(), calls=%async_computation.26 | async-start | bytes 737280
  856.0 233.2 %copy-start.44 = (f32[150]{0:T(256)S(1)}, f32[150]{0:T(256)}, u32[]{:S(2)}) copy-start(f32[150]{0:T(256)} %copy-done.43) | copy-start | bytes 1804
  1088.4 410.8 %reduce-scatter.31.cloned.1.call-start = ((), (), s32[]{:S(2)}) async-start(), calls=%async_computation.19 | async-start | bytes 737280 | tf_op jit(solution)/shard_map/reduce_scatter | solution.py:301
  1297.8 203.0 %reduce-scatter.37.cloned.1.call-start = ((), (), s32[]{:S(2)}) async-start(), calls=%async_computation.24 | async-start | bytes 737280
  (76 other events, 368.2 us)
Sparse Core Ops, SparseCore 0:
  19.2 40.1 all-gather.4
  61.0 37.4 all-gather.2
  387.7 32.5 all-reduce.13
  424.1 69.3 reduce-scatter.34
  497.3 68.0 reduce-scatter.26
  744.0 47.5 reduce-scatter.20
  794.1 47.8 reduce-scatter.22
  845.8 71.9 all-reduce.15
  921.4 162.6 reduce-scatter.32
  1087.0 18.8 reduce-scatter.42
  1108.9 19.7 reduce-scatter.38
  1132.1 163.4 reduce-scatter.28
  1299.3 128.1 reduce-scatter.24
  1430.0 21.0 reduce-scatter.40
  1453.6 22.0 reduce-scatter.30
  1478.2 22.0 reduce-scatter.36
